TPU v7x, 512 devices: a whole 4x4x16 slice. The times are simulated.
512 devices in a mesh: dp: 16 (over y, x_lo, core), tensor: 32 (over x_hi, z).
Axes of the slice: x: 4 (x_hi: 2, x_lo: 2; x = x_hi * 2 + x_lo), y: 4, z: 16, core: 2. Of those that a mesh axis runs over, the one named last changes fastest.
Arguments:
- hidden_pre: bfloat16 [2048, 24576], P('dp', 'tensor'), may hold values from -6 to 6
- out_grad: bfloat16 [2048, 6144], P('dp', 'tensor'), may hold values from -0.890625 to 0.890625
- down_weight: bfloat16 [24576, 6144], P('tensor', 'dp'), may hold values from -0.078125 to 0.078125
Outputs:
- grad_hidden: bfloat16 [2048, 24576], P('dp', 'tensor')
- grad_weight: bfloat16 [24576, 6144], P('tensor', 'dp')
All inputs are finite; a program needn't handle non-finite values.
Results may differ from a plain program's by a relative error of at most 0.019.
Values may be sent and summed in bfloat16 or wider, within the bound.
A program may use at most 64 MiB of HBM per device.

v0:
```python
import math

import jax
import jax.numpy as jnp
from jax import lax
from jax.sharding import PartitionSpec as P

coef = math.sqrt(2.0 / math.pi)


def gelu_parts(value):
    inner = coef * (value + 0.044715 * value * value * value)
    tval = jnp.tanh(inner)
    act = 0.5 * value * (1.0 + tval)
    slope = 0.5 * (1.0 + tval) + 0.5 * value * (1.0 - tval * tval) * coef * (
        1.0 + 3.0 * 0.044715 * value * value
    )
    return (act, slope)


def local(hidden_pre, out_grad, down_weight):
    group_grad = lax.all_gather(out_grad, "tensor", axis=1, tiled=True)
    owned_grad = lax.all_to_all(group_grad, "dp", split_axis=1, concat_axis=0, tiled=True)
    width = down_weight.shape[1]
    own_act, slope = gelu_parts(hidden_pre.astype(jnp.float32))
    piece = lax.all_gather(down_weight, "dp", axis=1, tiled=True)
    count = piece.shape[1] // width
    cols = group_grad
    cols = cols.reshape(cols.shape[0], count, width)
    rows = piece.reshape(piece.shape[0], count, width)
    parts = jnp.einsum("tkb,fkb->ktf", cols, rows, preferred_element_type=jnp.float32)
    summed = jnp.sum(parts.astype(jnp.bfloat16).astype(jnp.float32), axis=0)
    grad_hidden = (slope * summed).astype(jnp.bfloat16)
    activated = own_act.astype(jnp.bfloat16)
    rows = owned_grad
    grad_weight = lax.dot_general(
        lax.all_gather(activated, "dp", axis=0, tiled=True),
        rows,
        (((0,), (0,)), ((), ())),
        preferred_element_type=jnp.float32,
    )
    return (grad_hidden, grad_weight.astype(jnp.bfloat16))


def solution(mesh):
    placed = (P("dp", "tensor"), P("dp", "tensor"), P("tensor", "dp"))
    return jax.shard_map(
        local,
        mesh=mesh,
        in_specs=placed,
        out_specs=(P("dp", "tensor"), P("tensor", "dp")),
        check_vma=False,
    )
```

profile of v0, /device:TPU:1, one launch (start us, length us, event | category | flops | bytes accessed | tf_op | source)
XLA Modules:
  0.0 291.9 jit_solution(8519977791654980520)
XLA Ops:
  7.2 0.0 all-gather.4.cloned.1.call-start
  7.2 0.7 all-gather.4.cloned.1.call-update
  7.9 0.0 all-gather.6.cloned.1.call-start
  7.9 2.1 copy.8
  10.1 0.0 all-gather.6.cloned.1.call-update
  10.1 0.0 all-gather.8.cloned.1.call-start
  10.1 143.7 %all-gather.4.cloned.1.call-done = bf16[128,6144]{0,1:T(8,128)(2,1)} async-done(((bf16[128,192]{0,1:T(8,128)(2,1)}), bf16[128,6144]{0,1:T(8,128)(2,1)}) %all-gather.4.cloned.1.call-update) | async-done | bytes 1572880 | tf_op jit(solution)/shard_map/all_gather | solution.py:22
  153.8 71.5 %all-gather.6.cloned.1.call-done = bf16[768,6144]{0,1:T(8,128)(2,1)} async-done(((bf16[768,384]{0,1:T(8,128)(2,1)}), bf16[768,6144]{0,1:T(8,128)(2,1)}) %all-gather.6.cloned.1.call-update) | async-done | bytes 9437200 | tf_op jit(solution)/shard_map/all_gather | solution.py:26
  225.3 0.0 copy-start.1
  225.3 0.0 copy-start
  225.3 6.2 %convert_reduce_fusion = f32[128,768]{1,0:T(8,128)S(1)} fusion(bf16[128,16,384]{0,2,1:T(8,128)(2,1)} %bitcast.9, bf16[768,16,384]{0,2,1:T(8,128)(2,1)} %bitcast.8), kind=kOutput, calls=%fused_computation | convolution fusion | flops 1212579840 | bytes 11403264 | tf_op jit(solution)/shard_map/tkb,fkb->ktf/dot_general | solution.py:31
  231.4 0.0 copy-done.1
  231.4 1.0 fusion.7
  232.5 0.0 all-gather.8.cloned.1.call-update
  232.5 0.0 copy-done
  232.5 28.9 %all_to_all.16 = bf16[128,16,384]{0,2,1:T(8,128)(2,1)S(1)} all-to-all(bf16[128,16,384]{0,2,1:T(8,128)(2,1)S(1)} %bitcast.10), channel_id=1, replica_groups=mesh['dp'=16,'tensor'=32] {'dp'}, dimensions={1} | all-to-all | bytes 3145728 | tf_op jit(solution)/shard_map/all_to_all | solution.py:23
  261.4 0.9 copy.11
  262.2 18.6 %all-gather.8.cloned.1.call-done = bf16[2048,768]{1,0:T(8,128)(2,1)} async-done(((bf16[128,768]{1,0:T(8,128)(2,1)}), bf16[2048,768]{1,0:T(8,128)(2,1)}) %all-gather.8.cloned.1.call-update) | async-done | bytes 3145744 | tf_op jit(solution)/shard_map/all_gather | solution.py:37
  280.8 4.5 %convolution_convert_fusion = bf16[768,384]{1,0:T(8,128)(2,1)} fusion(bf16[2048,768]{1,0:T(8,128)(2,1)} %all-gather.8.cloned.1.call-done, bf16[2048,384]{1,0:T(8,128)(2,1)S(1)} %bitcast.12), kind=kOutput, calls=%fused_computation.1 | convolution fusion | flops 1208254464 | bytes 5308416 | tf_op jit(solution)/shard_map/dot_general | solution.py:36
Async XLA Ops:
  7.2 146.6 %all-gather.4.cloned.1.call-start = ((), (), s32[]{:S(2)}) async-start(), calls=%async_computation.1 | async-start | bytes 1622016 | tf_op jit(solution)/shard_map/all_gather | solution.py:22
  7.9 217.4 %all-gather.6.cloned.1.call-start = ((), (), s32[]{:S(2)}) async-start(), calls=%async_computation.2 | async-start | bytes 10027008 | tf_op jit(solution)/shard_map/all_gather | solution.py:26
  10.1 270.7 %all-gather.8.cloned.1.call-start = ((), (), s32[]{:S(2)}) async-start(), calls=%async_computation.3 | async-start | bytes 3342336 | tf_op jit(solution)/shard_map/all_gather | solution.py:37
  225.3 6.2 %copy-start.1 = (bf16[128,768]{1,0:T(8,128)(2,1)S(1)}, bf16[128,768]{1,0:T(8,128)(2,1)}, u32[]{:S(2)}) copy-start(bf16[128,768]{1,0:T(8,128)(2,1)} %param.3) | copy-start | bytes 589828
  225.3 7.2 %copy-start = (bf16[128,6144]{0,1:T(8,128)(2,1)S(1)}, bf16[128,6144]{0,1:T(8,128)(2,1)}, u32[]{:S(2)}) copy-start(bf16[128,6144]{0,1:T(8,128)(2,1)} %all-gather.4.cloned.1.call-done) | copy-start | bytes 4718596
Sparse Core Ops, SparseCore 0:
  11.1 142.6 all-gather.3
  156.5 68.7 all-gather.5
  232.6 48.1 all-gather.7
where the time goes:
time: 292 us
  waiting for transfers between devices  234 us (80%)
  blocking collectives  28.9 us (10%)
  between operations  13.8 us (5%)
  matrix products  10.7 us (4%)
  local copies, waits for them, and re-layouts  2.99 us (1%)
    all_gather x1, waiting for transfers between devices, local(): group_grad = lax.all_gather(out_grad, 'tensor', axis=1, tiled=True)  144 us
    all_gather x1, waiting for transfers between devices, local(): piece = lax.all_gather(down_weight, 'dp', axis=1, tiled=True)  71.5 us
    all_to_all x1, blocking collectives, local(): lax.all_to_all(group_grad, 'dp', split_axis=1, concat_axis=0, tiled=True)  28.9 us
    all_gather x1, waiting for transfers between devices, local(): lax.all_gather(activated, 'dp', axis=0, tiled=True)  18.6 us
    dot_general x1, matrix products, local(): jnp.einsum('tkb,fkb->ktf', cols, rows, preferred_element_type=jnp.float32)  6.15 us
  transfers between devices with their start and end apart: 3, of which 3 were waited for; matrix products, arithmetic and copies ran while one was open for 1% of the time, Pallas kernels for 0%

commit v1 on v0

v1 whole, which is shorter than its diff:
```python
import math

import jax
import jax.numpy as jnp
from jax import lax
from jax.experimental import pallas as pl
from jax.experimental.pallas import tpu as pltpu
from jax.sharding import PartitionSpec as P

coef = math.sqrt(2.0 / math.pi)
MESH = pl.DeviceIdType.MESH
NY, NX, NZ = 4, 2, 16
NQ = NY * NX


def gelu_parts(value):
    inner = coef * (value + 0.044715 * value * value * value)
    tval = jnp.tanh(inner)
    act = 0.5 * value * (1.0 + tval)
    slope = 0.5 * (1.0 + tval) + 0.5 * value * (1.0 - tval * tval) * coef * (
        1.0 + 3.0 * 0.044715 * value * value
    )
    return (act, slope)


def kernel(
    hid_hbm, grad_hbm, w_hbm, gh_ref, gw_ref,
    hid, wts, cols, cols_sib, act_own, act_sib, slope, stage, parts,
    loc_sem, w_sem, g_send, g_recv, right_send, right_recv, left_send, left_recv,
    gs_send, gs_recv, ax_sem, ay_send, ay_recv, ah_send, ah_recv, as_send, as_recv,
    rs_send, rs_recv,
):
    rem, div = lax.rem, lax.div
    dp = lax.axis_index("dp")
    tn = lax.axis_index("tensor")
    core, chip = rem(dp, 2), div(dp, 2)
    cy, cx = div(chip, NX), rem(chip, NX)
    cz, ch = rem(tn, NZ), div(tn, NZ)
    sib = dp + 1 - 2 * core

    def chip_at(y, x):
        return rem(y, NY) * NX + rem(x, NX)

    def block_at(j):
        return chip_at(cy + div(j, NX), cx + rem(j, NX))

    def at(dp_to, tn_to):
        return (dp_to, tn_to)

    def slot_at(place):
        j = div(place, 2)
        return block_at(j), rem(place, 2)

    to_chip, to_half, to_part = div(tn, 4), rem(div(tn, 2), 2), rem(tn, 2)
    to_j = rem(cy - div(to_chip, NX) + NY, NY) * NX + rem(cx - rem(to_chip, NX) + NX, NX)
    to_dp = to_chip * 2 + core
    to_z = to_j * 2 + to_half
    my_block, my_half = slot_at(cz)
    from_dp = my_block * 2 + core

    cp_hid = pltpu.make_async_copy(hid_hbm, hid, loc_sem.at[0])
    cp_w = pltpu.make_async_copy(w_hbm, wts.at[core], loc_sem.at[1])
    cp_hid.start()
    cp_w.start()

    barrier = pltpu.get_barrier_semaphore()
    expect = jnp.int32(0)
    for part in range(2):
        from_tn = chip * 4 + my_half * 2 + part
        here = jnp.logical_and(from_dp == dp, from_tn == tn)

        @pl.when(jnp.logical_not(here))
        def _():
            pl.semaphore_signal(barrier, inc=1, device_id=at(from_dp, from_tn), device_id_type=MESH)

    up = ch * NZ + rem(cz + 1, NZ)
    down = ch * NZ + rem(cz + NZ - 1, NZ)
    for other in (up, down):
        pl.semaphore_signal(barrier, inc=1, device_id=at(dp, other), device_id_type=MESH)
    pl.semaphore_signal(barrier, inc=1, device_id=at(sib, tn), device_id_type=MESH)
    for j in range(1, NQ):
        pl.semaphore_signal(barrier, inc=1, device_id=at(block_at(j) * 2 + core, tn), device_id_type=MESH)
    expect = jnp.int32(2 + 1 + NQ - 1)
    for half in range(2):
        away = jnp.logical_or(to_dp != dp, half * NZ + to_z != tn)
        expect = expect + away.astype(jnp.int32)
    pl.semaphore_wait(barrier, expect)

    def g_copy(half):
        return pltpu.make_async_remote_copy(
            src_ref=grad_hbm,
            dst_ref=cols.at[chip, to_half, pl.ds(pl.multiple_of(to_part * 192, 64), 192)],
            send_sem=g_send.at[half], recv_sem=g_recv.at[to_part],
            device_id=at(to_dp, half * NZ + to_z), device_id_type=MESH,
        )

    def g_local(half):
        return pltpu.make_async_copy(
            grad_hbm,
            cols.at[chip, to_half, pl.ds(pl.multiple_of(to_part * 192, 64), 192)],
            g_recv.at[to_part],
        )

    for half in range(2):
        away = jnp.logical_or(to_dp != dp, half * NZ + to_z != tn)

        @pl.when(away)
        def _():
            g_copy(half).start()

        @pl.when(jnp.logical_not(away))
        def _():
            g_local(half).start()

    cp_w.wait()
    w_copy = pltpu.make_async_remote_copy(
        src_ref=wts.at[core], dst_ref=wts.at[core], send_sem=w_sem.at[0], recv_sem=w_sem.at[1],
        device_id=at(sib, tn), device_id_type=MESH,
    )
    w_copy.start()

    cp_hid.wait()
    act, slp = gelu_parts(hid[...].astype(jnp.float32))
    act_own[chip] = act.astype(jnp.bfloat16)
    slope[...] = slp

    started = []

    def send(src, dst, send_sem, recv_sem, dp_to):
        copy = pltpu.make_async_remote_copy(
            src_ref=src, dst_ref=dst, send_sem=send_sem, recv_sem=recv_sem,
            device_id=at(dp_to, tn), device_id_type=MESH,
        )
        copy.start()
        started.append(copy)
        return copy

    def got(dst, recv_sem):
        pltpu.make_async_remote_copy(
            src_ref=dst, dst_ref=dst, send_sem=recv_sem, recv_sem=recv_sem,
            device_id=at(sib, tn), device_id_type=MESH,
        ).wait_recv()

    x_chip = chip_at(cy, cx + 1)

    def act_to_y(x_off, block):
        for k, off in ((0, 1), (1, 3)):
            dest = chip_at(cy + off, cx) * 2 + core
            send(act_own.at[block], act_own.at[block], ay_send.at[x_off, k], ay_recv.at[x_off, k], dest)

    def act_to_sib(j):
        block = block_at(j)
        send(act_own.at[block], act_sib.at[block], as_send.at[j], as_recv.at[j], sib)

    send(act_own.at[chip], act_own.at[chip], ax_sem.at[0], ax_sem.at[1], x_chip * 2 + core)
    act_to_y(0, chip)
    act_to_sib(0)

    def act_from_y(x_off):
        for k, off in ((0, 3), (1, 1)):
            block = chip_at(cy + off, cx + x_off)
            got(act_own.at[block], ay_recv.at[x_off, k])
            rows = pl.ds(k * 64, 64)
            dest = chip_at(cy + (1 if k == 0 else 3), cx) * 2 + core
            send(act_own.at[block, rows], act_own.at[block, rows],
                 ah_send.at[x_off, k], ah_recv.at[x_off, k], dest)
            act_to_sib(off * NX + x_off)

    def act_halves(x_off):
        block = chip_at(cy + 2, cx + x_off)
        for k in range(2):
            got(act_own.at[block, pl.ds(k * 64, 64)], ah_recv.at[x_off, k])
        act_to_sib(2 * NX + x_off)

    for part in range(2):
        got(cols.at[my_block, my_half, pl.ds(part * 192, 192)], g_recv.at[part])

    def ring(place, tn_to, send_sem, recv_sem):
        block, half = slot_at(place)
        copy = pltpu.make_async_remote_copy(
            src_ref=cols.at[block, half], dst_ref=cols.at[block, half],
            send_sem=send_sem, recv_sem=recv_sem, device_id=at(dp, tn_to), device_id_type=MESH,
        )
        copy.start()
        started.append(copy)

    ring(cz, up, right_send.at[0], right_recv.at[0])
    ring(cz, down, left_send.at[0], left_recv.at[0])

    def partial(step):
        odd = rem(cz + step, 2)
        j = div(rem(cz + NZ + jnp.where(odd == 1, step, -step), NZ), 2)
        block = block_at(j)
        send(cols.at[block, 1 - core], cols_sib.at[block], gs_send.at[step - 1], gs_recv.at[block], sib)
        if step == 1:
            w_copy.wait_recv()
        value = jnp.dot(wts[0], cols[block, 0], preferred_element_type=jnp.float32)
        value += jnp.dot(wts[1], cols[block, 1], preferred_element_type=jnp.float32)
        value = value.astype(jnp.bfloat16)
        copy = pltpu.make_async_remote_copy(
            src_ref=stage.at[step - 1], dst_ref=parts.at[chip],
            send_sem=rs_send.at[step - 1], recv_sem=rs_recv.at[chip],
            device_id=at(block * 2 + core, tn), device_id_type=MESH,
        )

        @pl.when(block == chip)
        def _():
            parts[chip] = value

        @pl.when(block != chip)
        def _():
            stage[step - 1] = value
            copy.start()

        return block, copy

    rs = []
    for step in range(1, NZ // 2 + 1):
        place = rem(cz + NZ - step, NZ)
        block, half = slot_at(place)
        got(cols.at[block, half], right_recv.at[step - 1])
        if step < NZ // 2:
            ring(place, up, right_send.at[step], right_recv.at[step])
        if step < NZ // 2:
            place = rem(cz + step, NZ)
            block, half = slot_at(place)
            got(cols.at[block, half], left_recv.at[step - 1])
            if step < NZ // 2 - 1:
                ring(place, down, left_send.at[step], left_recv.at[step])
        rs.append(partial(step))
        if step == 1:
            got(act_own.at[x_chip], ax_sem.at[1])
            act_to_y(1, x_chip)
            act_to_sib(1)
        elif step == 2:
            act_from_y(0)
        elif step == 4:
            act_from_y(1)
        elif step == 5:
            act_halves(0)
        elif step == 7:
            act_halves(1)

    for j in range(NQ):
        got(act_sib.at[block_at(j)], as_recv.at[j])
    for block in range(NQ):
        got(cols_sib.at[block], gs_recv.at[block])
    lhs = jnp.concatenate([cols[block, core] for block in range(NQ)], axis=1)
    total = jnp.dot(lhs, act_own[...].reshape(NQ * 128, 768), preferred_element_type=jnp.float32)
    lhs = jnp.concatenate([cols_sib[block] for block in range(NQ)], axis=1)
    total += jnp.dot(lhs, act_sib[...].reshape(NQ * 128, 768), preferred_element_type=jnp.float32)
    gw_ref[...] = total.astype(jnp.bfloat16)

    for j in range(1, NQ):
        block = block_at(j)
        got(parts.at[block], rs_recv.at[block])
    summed = parts[0].astype(jnp.float32)
    for block in range(1, NQ):
        summed += parts[block].astype(jnp.float32)
    gh_ref[...] = (slope[...] * summed.T).astype(jnp.bfloat16)

    for half in range(2):
        @pl.when(jnp.logical_or(to_dp != dp, half * NZ + to_z != tn))
        def _():
            g_copy(half).wait_send()

    w_copy.wait_send()
    for copy in started:
        copy.wait_send()
    for block, copy in rs:
        @pl.when(block != chip)
        def _():
            copy.wait_send()


def local(hidden_pre, out_grad, down_weight):
    bf16, f32 = jnp.bfloat16, jnp.float32
    dma = pltpu.SemaphoreType.DMA
    half = NZ // 2
    grad_hidden, gw = pl.pallas_call(
        kernel,
        out_shape=(
            jax.ShapeDtypeStruct((128, 768), bf16),
            jax.ShapeDtypeStruct((384, 768), bf16),
        ),
        in_specs=[pl.BlockSpec(memory_space=pl.ANY)] * 3,
        out_specs=[pl.BlockSpec(memory_space=pltpu.VMEM)] * 2,
        scratch_shapes=[
            pltpu.VMEM((128, 768), bf16),
            pltpu.VMEM((2, 768, 384), bf16),
            pltpu.VMEM((NQ, 2, 384, 128), bf16),
            pltpu.VMEM((NQ, 384, 128), bf16),
            pltpu.VMEM((NQ, 128, 768), bf16),
            pltpu.VMEM((NQ, 128, 768), bf16),
            pltpu.VMEM((128, 768), f32),
            pltpu.VMEM((half, 768, 128), bf16),
            pltpu.VMEM((NQ, 768, 128), bf16),
            dma((2,)), dma((2,)), dma((2,)), dma((2,)),
            dma((half,)), dma((half,)), dma((half,)), dma((half,)),
            dma((half,)), dma((NQ,)), dma((2,)), dma((2, 2)), dma((2, 2)),
            dma((2, 2)), dma((2, 2)), dma((NQ,)), dma((NQ,)),
            dma((half,)), dma((NQ,)),
        ],
        compiler_params=pltpu.CompilerParams(
            collective_id=0, has_side_effects=True, vmem_limit_bytes=48 * 1024 * 1024
        ),
    )(hidden_pre, out_grad.T, down_weight)
    return (grad_hidden, gw.T)


def solution(mesh):
    placed = (P("dp", "tensor"), P("dp", "tensor"), P("tensor", "dp"))
    return jax.shard_map(
        local,
        mesh=mesh,
        in_specs=placed,
        out_specs=(P("dp", "tensor"), P("tensor", "dp")),
        check_vma=False,
    )
```

time: 292 us -> 87.7 us (0.30)
  the two profiles are of different devices: /device:TPU:1 before, /device:TPU:12 now
where the time goes in v1:
time: 87.7 us; the launch traced here: 87.4 us
  Pallas kernels  82.3 us (94%)
  local copies, waits for them, and re-layouts  4.51 us (5%)
    pallas_call x1, Pallas kernels, local(): pl.pallas_call(kernel, out_shape=(jax.ShapeDtypeStruct((128, 768), bf16),...  82.3 us
    unnamed x8, local copies, waits for them, and re-layouts  4.51 us

profile of v1, /device:TPU:12, one launch (start us, length us, event | category | flops | bytes accessed | tf_op | source)
XLA Modules:
  0.0 87.4 jit_solution(1911973447273944032)
XLA Ops:
  0.6 0.0 copy-start
  0.6 1.1 %copy-done = bf16[768,384]{1,0:T(8,128)(2,1)S(1)} copy-done((bf16[768,384]{1,0:T(8,128)(2,1)S(1)}, bf16[768,384]{1,0:T(8,128)(2,1)}, u32[]{:S(2)}) %copy-start) | copy-done | bytes 589848
  1.7 0.0 copy-start.1
  1.7 0.9 %copy-done.1 = bf16[128,768]{1,0:T(8,128)(2,1)S(1)} copy-done((bf16[128,768]{1,0:T(8,128)(2,1)S(1)}, bf16[128,768]{1,0:T(8,128)(2,1)}, u32[]{:S(2)}) %copy-start.1) | copy-done | bytes 196632
  2.6 0.0 copy-start.2
  2.6 0.8 copy-done.2
  3.4 82.3 %shard_map.50 = (bf16[128,768]{1,0:T(8,128)(2,1)S(1)}, bf16[384,768]{1,0:T(8,128)(2,1)S(1)}) custom-call(bf16[128,768]{1,0:T(8,128)(2,1)S(1)} %copy-done.1, bf16[192,128]{1,0:T(8,128)(2,1)S(1)} %bitcast.3, bf16[768,384]{1,0:T(8,128)(2,1)S(1)} %copy-done), custom_call_target="tpu_custom_call" | custom-call | tf_op jit(solution)/shard_map/pallas_call | solution.py:280
  85.7 1.1 %copy.5 = bf16[768,384]{1,0:T(8,128)(2,1)} copy(bf16[768,384]{0,1:T(8,128)(2,1)S(1)} %bitcast.2) | data formatting | bytes 1179648
  86.7 0.7 copy.7
Async XLA Ops:
  0.6 1.1 %copy-start = (bf16[768,384]{1,0:T(8,128)(2,1)S(1)}, bf16[768,384]{1,0:T(8,128)(2,1)}, u32[]{:S(2)}) copy-start(bf16[768,384]{1,0:T(8,128)(2,1)} %w_hbm.1) | copy-start | bytes 1769476
  1.7 0.9 %copy-start.1 = (bf16[128,768]{1,0:T(8,128)(2,1)S(1)}, bf16[128,768]{1,0:T(8,128)(2,1)}, u32[]{:S(2)}) copy-start(bf16[128,768]{1,0:T(8,128)(2,1)} %hid_hbm.1) | copy-start | bytes 589828
  2.6 0.8 copy-start.2

commit v2 on v0

v2 whole, which is shorter than its diff:
```python
import math

import jax
import jax.numpy as jnp
from jax import lax
from jax.experimental import pallas as pl
from jax.experimental.pallas import tpu as pltpu
from jax.sharding import PartitionSpec as P

coef = math.sqrt(2.0 / math.pi)
MESH = pl.DeviceIdType.MESH
NY, NX, NZ = 4, 2, 16
NQ = NY * NX


def gelu_parts(value):
    inner = coef * (value + 0.044715 * value * value * value)
    tval = jnp.tanh(inner)
    act = 0.5 * value * (1.0 + tval)
    slope = 0.5 * (1.0 + tval) + 0.5 * value * (1.0 - tval * tval) * coef * (
        1.0 + 3.0 * 0.044715 * value * value
    )
    return (act, slope)


def kernel(
    hid_hbm, grad_hbm, w_hbm, gh_ref, gw_ref,
    hid, wts, cols, cols_sib, act_own, act_sib, slope, first, second, comb, x_parts, y_parts,
    loc_sem, w_sem, g_sem, peer_sem, right_send, right_recv, left_send, left_recv,
    gs_send, gs_recv, ax_sem, ay_send, ay_recv, ah_send, ah_recv, as_send, as_recv,
    x_send, x_recv, y_send, y_recv,
):
    rem, div = lax.rem, lax.div
    dp = lax.axis_index("dp")
    tn = lax.axis_index("tensor")
    core, chip = rem(dp, 2), div(dp, 2)
    cy, cx = div(chip, NX), rem(chip, NX)
    cz, ch = rem(tn, NZ), div(tn, NZ)
    sib = dp + 1 - 2 * core

    def chip_at(dy, dx):
        return rem(cy + dy, NY) * NX + rem(cx + dx, NX)

    def block_at(j):
        return chip_at(div(j, NX), rem(j, NX))

    def at(dp_to, tn_to):
        return (dp_to, tn_to)

    def peer_at(dy, dx):
        return at(chip_at(dy, dx) * 2 + core, tn)

    def slot_at(place):
        return block_at(div(place, 2)), rem(place, 2)

    def piece(place, part):
        block, half = slot_at(place)
        return cols.at[block, half, pl.ds(pl.multiple_of(part * 192, 64), 192)]

    to_chip, to_half, to_part = div(tn, 4), rem(div(tn, 2), 2), rem(tn, 2)
    to_j = rem(cy - div(to_chip, NX) + NY, NY) * NX + rem(cx - rem(to_chip, NX) + NX, NX)
    to_dp = to_chip * 2 + core
    to_tn = to_part * NZ + to_j * 2 + to_half
    from_dp = slot_at(cz)[0] * 2 + core
    from_tn = chip * 4 + rem(cz, 2) * 2 + ch
    to_away = jnp.logical_or(to_dp != dp, to_tn != tn)
    from_away = jnp.logical_or(from_dp != dp, from_tn != tn)

    lead = div(cz, 4)
    turn = 1 - 2 * rem(div(cz, 2), 2)
    order = [lead, rem(lead + NY - turn, NY), rem(lead + NY + turn, NY), rem(lead + 2, NY)]
    last = order[3]

    up = at(dp, ch * NZ + rem(cz + 1, NZ))
    down = at(dp, ch * NZ + rem(cz + NZ - 1, NZ))
    across = at(dp, rem(tn + NZ, 2 * NZ))
    beside = at(sib, tn)

    barrier = pltpu.get_barrier_semaphore()
    greet = [up, down, across, beside, peer_at(0, 1), peer_at(NY - last, 1)]
    greet += [peer_at(dy, 0) for dy in range(1, NY)]
    for other in greet:
        pl.semaphore_signal(barrier, inc=1, device_id=other, device_id_type=MESH)

    @pl.when(from_away)
    def _():
        pl.semaphore_signal(barrier, inc=1, device_id=at(from_dp, from_tn), device_id_type=MESH)

    cp_hid = pltpu.make_async_copy(hid_hbm, hid, loc_sem.at[0])
    cp_w = pltpu.make_async_copy(w_hbm, wts.at[core], loc_sem.at[1])
    cp_hid.start()
    cp_w.start()
    cp_hid.wait()
    act, slp = gelu_parts(hid[...].astype(jnp.float32))
    act_own[chip] = act.astype(jnp.bfloat16)
    slope[...] = slp
    cp_w.wait()
    pl.semaphore_wait(barrier, len(greet) + to_away.astype(jnp.int32))

    started = []

    def send(src, dst, send_sem, recv_sem, dest, keep=True):
        copy = pltpu.make_async_remote_copy(
            src_ref=src, dst_ref=dst, send_sem=send_sem, recv_sem=recv_sem,
            device_id=dest, device_id_type=MESH,
        )
        copy.start()
        if keep:
            started.append(copy)

    def got(dst, recv_sem):
        pltpu.make_async_remote_copy(
            src_ref=dst, dst_ref=dst, send_sem=recv_sem, recv_sem=recv_sem,
            device_id=beside, device_id_type=MESH,
        ).wait_recv()

    def sent(src, send_sem):
        pltpu.make_async_remote_copy(
            src_ref=src, dst_ref=src, send_sem=send_sem, recv_sem=send_sem,
            device_id=beside, device_id_type=MESH,
        ).wait_send()

    g_dst = cols.at[chip, to_half, pl.ds(pl.multiple_of(to_part * 192, 64), 192)]

    @pl.when(to_away)
    def _():
        send(grad_hbm, g_dst, g_sem.at[0], g_sem.at[1], at(to_dp, to_tn), keep=False)

    @pl.when(jnp.logical_not(to_away))
    def _():
        pltpu.make_async_copy(grad_hbm, g_dst, g_sem.at[1]).start()

    def act_to_y(dx):
        block = chip_at(0, dx)
        for k, dy in ((0, 1), (1, NY - 1)):
            send(act_own.at[block], act_own.at[block], ay_send.at[dx, k], ay_recv.at[dx, k], peer_at(dy, 0))

    def act_to_sib(j):
        block = block_at(j)
        send(act_own.at[block], act_sib.at[block], as_send.at[j], as_recv.at[j], beside)

    def act_from_y(dx):
        for k, dy in ((0, NY - 1), (1, 1)):
            block = chip_at(dy, dx)
            got(act_own.at[block], ay_recv.at[dx, k])
            rows = pl.ds(k * 64, 64)
            send(act_own.at[block, rows], act_own.at[block, rows],
                 ah_send.at[dx, k], ah_recv.at[dx, k], peer_at(NY - dy, 0))
            act_to_sib(dy * NX + dx)

    def act_halves(dx):
        block = chip_at(2, dx)
        for k in range(2):
            got(act_own.at[block, pl.ds(k * 64, 64)], ah_recv.at[dx, k])
        act_to_sib(2 * NX + dx)

    send(wts.at[core], wts.at[core], w_sem.at[0], w_sem.at[1], beside)
    send(act_own.at[chip], act_own.at[chip], ax_sem.at[0], ax_sem.at[1], peer_at(0, 1))
    act_to_y(0)
    act_to_sib(0)

    pieces = (ch, 1 - ch)

    def right(step, n):
        ref = piece(rem(cz + NZ - step, NZ), pieces[n])
        if step > 0:
            got(ref, right_recv.at[n, step - 1])
        if step < NZ // 2:
            send(ref, ref, right_send.at[n, step], right_recv.at[n, step], up)

    def left(step, n):
        ref = piece(rem(cz + step, NZ), pieces[n])
        if step > 0:
            got(ref, left_recv.at[n, step - 1])
        if step < NZ // 2 - 1:
            send(ref, ref, left_send.at[n, step], left_recv.at[n, step], down)

    got(piece(cz, ch), g_sem.at[1])
    right(0, 0)
    left(0, 0)
    send(piece(cz, ch), piece(cz, ch), peer_sem.at[0], peer_sem.at[1], across)
    got(piece(cz, 1 - ch), peer_sem.at[1])
    right(0, 1)
    left(0, 1)

    def partial(step):
        odd = rem(cz + step, 2)
        j = div(rem(cz + NZ + jnp.where(odd == 1, step, -step), NZ), 2)
        dy, dx = div(j, NX), rem(j, NX)
        block = block_at(j)
        send(cols.at[block, 1 - core], cols_sib.at[block], gs_send.at[step - 1], gs_recv.at[block], beside)
        if step == 1:
            got(wts.at[1 - core], w_sem.at[1])
        value = jnp.dot(wts[0], cols[block, 0], preferred_element_type=jnp.float32)
        value += jnp.dot(wts[1], cols[block, 1], preferred_element_type=jnp.float32)
        value = value.astype(jnp.bfloat16)
        final = (dy == last).astype(jnp.int32)

        @pl.when(dx == 1)
        def _():
            second[dy] = value
            send(second.at[dy], x_parts.at[dy], x_send.at[dy], x_recv.at[dy], peer_at(final * dy, 1), keep=False)

        @pl.when(jnp.logical_and(dx == 0, jnp.logical_or(final == 0, dy != 0)))
        def _():
            first[dy] = value

        @pl.when(jnp.logical_and(jnp.logical_and(dx == 0, final == 1), dy != 0))
        def _():
            send(first.at[dy], y_parts.at[dy], y_send.at[dy], y_recv.at[dy], peer_at(dy, 0), keep=False)

        @pl.when(jnp.logical_and(jnp.logical_and(dx == 0, final == 1), dy == 0))
        def _():
            y_parts[0] = value

    def combine(i):
        dy = order[i]
        got(x_parts.at[dy], x_recv.at[dy])
        value = (first[dy].astype(jnp.float32) + x_parts[dy].astype(jnp.float32)).astype(jnp.bfloat16)

        @pl.when(dy == 0)
        def _():
            y_parts[0] = value

        @pl.when(dy != 0)
        def _():
            comb[i] = value
            send(comb.at[i], y_parts.at[dy], y_send.at[dy], y_recv.at[dy], peer_at(dy, 0), keep=False)

    for step in range(1, NZ // 2 + 1):
        for n in range(2):
            right(step, n)
            if step < NZ // 2:
                left(step, n)
        partial(step)
        if step == 1:
            got(act_own.at[chip_at(0, 1)], ax_sem.at[1])
            act_to_y(1)
            act_to_sib(1)
        elif step == 2:
            act_from_y(0)
        elif step == 4:
            combine(0)
            act_from_y(1)
        elif step == 5:
            act_halves(0)
        elif step == 6:
            combine(1)
        elif step == 7:
            act_halves(1)
        elif step == 8:
            combine(2)

    lhs = jnp.concatenate([cols[block, core] for block in range(NQ)], axis=1)
    total = jnp.dot(lhs, act_own[...].reshape(NQ * 128, 768), preferred_element_type=jnp.float32)
    for j in range(NQ):
        got(act_sib.at[block_at(j)], as_recv.at[j])
    for block in range(NQ):
        got(cols_sib.at[block], gs_recv.at[block])
    lhs = jnp.concatenate([cols_sib[block] for block in range(NQ)], axis=1)
    total += jnp.dot(lhs, act_sib[...].reshape(NQ * 128, 768), preferred_element_type=jnp.float32)
    gw_ref[...] = total.astype(jnp.bfloat16)

    for dy in range(1, NY):
        got(y_parts.at[dy], y_recv.at[dy])
    got(x_parts.at[last], x_recv.at[last])
    summed = x_parts[last].astype(jnp.float32)
    for dy in range(NY):
        summed += y_parts[dy].astype(jnp.float32)
    gh_ref[...] = (slope[...] * summed.T).astype(jnp.bfloat16)

    @pl.when(to_away)
    def _():
        sent(grad_hbm, g_sem.at[0])

    for copy in started:
        copy.wait_send()
    for dy in range(NY):
        sent(second.at[dy], x_send.at[dy])
    for dy in range(1, NY):
        sent(comb.at[0], y_send.at[dy])


def local(hidden_pre, out_grad, down_weight):
    bf16, f32 = jnp.bfloat16, jnp.float32
    dma = pltpu.SemaphoreType.DMA
    half = NZ // 2
    grad_hidden, gw = pl.pallas_call(
        kernel,
        out_shape=(
            jax.ShapeDtypeStruct((128, 768), bf16),
            jax.ShapeDtypeStruct((384, 768), bf16),
        ),
        in_specs=[pl.BlockSpec(memory_space=pl.ANY)] * 3,
        out_specs=[pl.BlockSpec(memory_space=pltpu.VMEM)] * 2,
        scratch_shapes=[
            pltpu.VMEM((128, 768), bf16),
            pltpu.VMEM((2, 768, 384), bf16),
            pltpu.VMEM((NQ, 2, 384, 128), bf16),
            pltpu.VMEM((NQ, 384, 128), bf16),
            pltpu.VMEM((NQ, 128, 768), bf16),
            pltpu.VMEM((NQ, 128, 768), bf16),
            pltpu.VMEM((128, 768), f32),
            pltpu.VMEM((NY, 768, 128), bf16),
            pltpu.VMEM((NY, 768, 128), bf16),
            pltpu.VMEM((NY - 1, 768, 128), bf16),
            pltpu.VMEM((NY, 768, 128), bf16),
            pltpu.VMEM((NY, 768, 128), bf16),
            dma((2,)), dma((2,)), dma((2,)), dma((2,)),
            dma((2, half)), dma((2, half)), dma((2, half)), dma((2, half)),
            dma((half,)), dma((NQ,)), dma((2,)), dma((2, 2)), dma((2, 2)),
            dma((2, 2)), dma((2, 2)), dma((NQ,)), dma((NQ,)),
            dma((NY,)), dma((NY,)), dma((NY,)), dma((NY,)),
        ],
        compiler_params=pltpu.CompilerParams(
            collective_id=0, has_side_effects=True, vmem_limit_bytes=60 * 1024 * 1024
        ),
    )(hidden_pre, out_grad.T, down_weight)
    return (grad_hidden, gw.T)


def solution(mesh):
    placed = (P("dp", "tensor"), P("dp", "tensor"), P("tensor", "dp"))
    return jax.shard_map(
        local,
        mesh=mesh,
        in_specs=placed,
        out_specs=(P("dp", "tensor"), P("tensor", "dp")),
        check_vma=False,
    )
```

time: 292 us -> 72.9 us (0.25)
  the two profiles are of different devices: /device:TPU:1 before, /device:TPU:8 now
where the time goes in v2:
time: 72.9 us; the launch traced here: 72.7 us
  Pallas kernels  69.2 us (95%)
  local copies, waits for them, and re-layouts  2.84 us (4%)
    pallas_call x1, Pallas kernels, local(): pl.pallas_call(kernel, out_shape=(jax.ShapeDtypeStruct((128, 768), bf16),...  69.2 us
    unnamed x4, local copies, waits for them, and re-layouts  2.84 us

profile of v2, /device:TPU:8, one launch (start us, length us, event | category | flops | bytes accessed | tf_op | source)
XLA Modules:
  0.0 72.7 jit_solution(2617489775082932905)
XLA Ops:
  0.6 69.2 %shard_map.50 = (bf16[128,768]{1,0:T(8,128)(2,1)}, bf16[384,768]{1,0:T(8,128)(2,1)}) custom-call(bf16[128,768]{1,0:T(8,128)(2,1)} %hid_hbm.1, bf16[192,128]{1,0:T(8,128)(2,1)} %bitcast.3, bf16[768,384]{1,0:T(8,128)(2,1)} %w_hbm.1), custom_call_target="tpu_custom_call" | custom-call | tf_op jit(solution)/shard_map/pallas_call | solution.py:288
  69.9 0.0 copy-start
  69.9 2.2 %copy.5 = bf16[768,384]{1,0:T(8,128)(2,1)} copy(bf16[768,384]{0,1:T(8,128)(2,1)} %bitcast.2) | data formatting | bytes 1179648
  72.0 0.0 copy-done
  72.0 0.7 copy.7
Async XLA Ops:
  69.9 2.2 %copy-start = (bf16[128,768]{1,0:T(8,128)(2,1)S(1)}, bf16[128,768]{1,0:T(8,128)(2,1)}, u32[]{:S(2)}) copy-start(bf16[128,768]{1,0:T(8,128)(2,1)} %get-tuple-element.10) | copy-start | bytes 589828

commit v3 on v2

--- a/solution.py
+++ b/solution.py
@@ -25,8 +25,8 @@
 
 def kernel(
     hid_hbm, grad_hbm, w_hbm, gh_ref, gw_ref,
-    hid, wts, cols, cols_sib, act_own, act_sib, slope, first, second, comb, x_parts, y_parts,
-    loc_sem, w_sem, g_sem, peer_sem, right_send, right_recv, left_send, left_recv,
+    hid, wts, cols, act_own, act_sib, slope, first, second, comb, x_parts, y_parts,
+    loc_sem, w_sem, g_send, g_recv, peer_send, peer_recv, hand_send, hand_recv, right_send, right_recv, left_send, left_recv,
     gs_send, gs_recv, ax_sem, ay_send, ay_recv, ah_send, ah_recv, as_send, as_recv,
     x_send, x_recv, y_send, y_recv,
 ):
@@ -53,18 +53,17 @@
     def slot_at(place):
         return block_at(div(place, 2)), rem(place, 2)
 
-    def piece(place, part):
+    def piece(par, place, part):
         block, half = slot_at(place)
-        return cols.at[block, half, pl.ds(pl.multiple_of(part * 192, 64), 192)]
+        return cols.at[par, block, half, pl.ds(pl.multiple_of(part * 192, 64), 192)]
 
     to_chip, to_half, to_part = div(tn, 4), rem(div(tn, 2), 2), rem(tn, 2)
     to_j = rem(cy - div(to_chip, NX) + NY, NY) * NX + rem(cx - rem(to_chip, NX) + NX, NX)
-    to_dp = to_chip * 2 + core
+    to_dp = to_chip * 2 + 1
     to_tn = to_part * NZ + to_j * 2 + to_half
-    from_dp = slot_at(cz)[0] * 2 + core
+    from_dp = slot_at(cz)[0] * 2
     from_tn = chip * 4 + rem(cz, 2) * 2 + ch
     to_away = jnp.logical_or(to_dp != dp, to_tn != tn)
-    from_away = jnp.logical_or(from_dp != dp, from_tn != tn)
 
     lead = div(cz, 4)
     turn = 1 - 2 * rem(div(cz, 2), 2)
@@ -77,14 +76,19 @@
     beside = at(sib, tn)
 
     barrier = pltpu.get_barrier_semaphore()
-    greet = [up, down, across, beside, peer_at(0, 1), peer_at(NY - last, 1)]
+    greet = [beside, peer_at(0, 1), peer_at(NY - last, 1)]
     greet += [peer_at(dy, 0) for dy in range(1, NY)]
     for other in greet:
         pl.semaphore_signal(barrier, inc=1, device_id=other, device_id_type=MESH)
 
-    @pl.when(from_away)
-    def _():
-        pl.semaphore_signal(barrier, inc=1, device_id=at(from_dp, from_tn), device_id_type=MESH)
+    @pl.when(core == 1)
+    def _():
+        for other in (up, down, across, at(from_dp, from_tn)):
+            pl.semaphore_signal(barrier, inc=1, device_id=other, device_id_type=MESH)
+
+        @pl.when(jnp.logical_or(from_dp + 1 != dp, from_tn != tn))
+        def _():
+            pl.semaphore_signal(barrier, inc=1, device_id=at(from_dp + 1, from_tn), device_id_type=MESH)
 
     cp_hid = pltpu.make_async_copy(hid_hbm, hid, loc_sem.at[0])
     cp_w = pltpu.make_async_copy(w_hbm, wts.at[core], loc_sem.at[1])
@@ -95,7 +99,7 @@
     act_own[chip] = act.astype(jnp.bfloat16)
     slope[...] = slp
     cp_w.wait()
-    pl.semaphore_wait(barrier, len(greet) + to_away.astype(jnp.int32))
+    pl.semaphore_wait(barrier, len(greet) + 3 * core + to_away.astype(jnp.int32))
 
     started = []
 
@@ -120,15 +124,15 @@
             device_id=beside, device_id_type=MESH,
         ).wait_send()
 
-    g_dst = cols.at[chip, to_half, pl.ds(pl.multiple_of(to_part * 192, 64), 192)]
+    g_dst = cols.at[core, chip, to_half, pl.ds(pl.multiple_of(to_part * 192, 64), 192)]
 
     @pl.when(to_away)
     def _():
-        send(grad_hbm, g_dst, g_sem.at[0], g_sem.at[1], at(to_dp, to_tn), keep=False)
+        send(grad_hbm, g_dst, g_send, g_recv.at[core], at(to_dp, to_tn), keep=False)
 
     @pl.when(jnp.logical_not(to_away))
     def _():
-        pltpu.make_async_copy(grad_hbm, g_dst, g_sem.at[1]).start()
+        pltpu.make_async_copy(grad_hbm, g_dst, g_recv.at[core]).start()
 
     def act_to_y(dx):
         block = chip_at(0, dx)
@@ -161,38 +165,80 @@
 
     pieces = (ch, 1 - ch)
 
-    def right(step, n):
-        ref = piece(rem(cz + NZ - step, NZ), pieces[n])
+    def right(step, n, par):
+        ref = piece(par, rem(cz + NZ - step, NZ), pieces[n])
         if step > 0:
-            got(ref, right_recv.at[n, step - 1])
+            got(ref, right_recv.at[par, n, step - 1])
         if step < NZ // 2:
-            send(ref, ref, right_send.at[n, step], right_recv.at[n, step], up)
-
-    def left(step, n):
-        ref = piece(rem(cz + step, NZ), pieces[n])
+            send(ref, ref, right_send.at[par, n, step], right_recv.at[par, n, step], up, keep=False)
+
+    def left(step, n, par):
+        ref = piece(par, rem(cz + step, NZ), pieces[n])
         if step > 0:
-            got(ref, left_recv.at[n, step - 1])
+            got(ref, left_recv.at[par, n, step - 1])
         if step < NZ // 2 - 1:
-            send(ref, ref, left_send.at[n, step], left_recv.at[n, step], down)
-
-    got(piece(cz, ch), g_sem.at[1])
-    right(0, 0)
-    left(0, 0)
-    send(piece(cz, ch), piece(cz, ch), peer_sem.at[0], peer_sem.at[1], across)
-    got(piece(cz, 1 - ch), peer_sem.at[1])
-    right(0, 1)
-    left(0, 1)
+            send(ref, ref, left_send.at[par, n, step], left_recv.at[par, n, step], down, keep=False)
+
+    def hand(way, step):
+        block, half = slot_at(rem(cz + NZ + (step if way else -step), NZ))
+        ref = cols.at[0, block, half]
+        send(ref, ref, hand_send.at[way, step], hand_recv.at[way, step], beside, keep=False)
+
+    def handed(way, step):
+        block, half = slot_at(rem(cz + NZ + (step if way else -step), NZ))
+        got(cols.at[0, block, half], hand_recv.at[way, step])
+
+    def ring(step):
+        @pl.when(core == 1)
+        def _():
+            for n in range(2):
+                for par in range(2):
+                    right(step, n, par)
+                    if step < NZ // 2:
+                        left(step, n, par)
+            hand(0, step)
+            if step < NZ // 2:
+                hand(1, step)
+
+        @pl.when(core == 0)
+        def _():
+            handed(0, step)
+            if step < NZ // 2:
+                handed(1, step)
+
+    @pl.when(core == 1)
+    def _():
+        for par in range(2):
+            ref = piece(par, cz, ch)
+            got(ref, g_recv.at[par])
+            right(0, 0, par)
+            left(0, 0, par)
+            send(ref, ref, peer_send.at[par], peer_recv.at[par], across, keep=False)
+        for par in range(2):
+            got(piece(par, cz, 1 - ch), peer_recv.at[par])
+            right(0, 1, par)
+            left(0, 1, par)
+        hand(0, 0)
+
+    @pl.when(core == 0)
+    def _():
+        handed(0, 0)
 
     def partial(step):
         odd = rem(cz + step, 2)
         j = div(rem(cz + NZ + jnp.where(odd == 1, step, -step), NZ), 2)
         dy, dx = div(j, NX), rem(j, NX)
         block = block_at(j)
-        send(cols.at[block, 1 - core], cols_sib.at[block], gs_send.at[step - 1], gs_recv.at[block], beside)
+
+        @pl.when(core == 1)
+        def _():
+            ref = cols.at[1, block, 0]
+            send(ref, ref, gs_send.at[step - 1], gs_recv.at[block], beside, keep=False)
+
         if step == 1:
             got(wts.at[1 - core], w_sem.at[1])
-        value = jnp.dot(wts[0], cols[block, 0], preferred_element_type=jnp.float32)
-        value += jnp.dot(wts[1], cols[block, 1], preferred_element_type=jnp.float32)
+        value = jnp.dot(wts[0], cols[core, block, 0], preferred_element_type=jnp.float32)
+        value += jnp.dot(wts[1], cols[core, block, 1], preferred_element_type=jnp.float32)
         value = value.astype(jnp.bfloat16)
         final = (dy == last).astype(jnp.int32)
 
@@ -228,10 +274,7 @@
             send(comb.at[i], y_parts.at[dy], y_send.at[dy], y_recv.at[dy], peer_at(dy, 0), keep=False)
 
     for step in range(1, NZ // 2 + 1):
-        for n in range(2):
-            right(step, n)
-            if step < NZ // 2:
-                left(step, n)
+        ring(step)
         partial(step)
         if step == 1:
             got(act_own.at[chip_at(0, 1)], ax_sem.at[1])
@@ -251,13 +294,17 @@
         elif step == 8:
             combine(2)
 
-    lhs = jnp.concatenate([cols[block, core] for block in range(NQ)], axis=1)
+    lhs = jnp.concatenate([cols[core, block, core] for block in range(NQ)], axis=1)
     total = jnp.dot(lhs, act_own[...].reshape(NQ * 128, 768), preferred_element_type=jnp.float32)
     for j in range(NQ):
         got(act_sib.at[block_at(j)], as_recv.at[j])
-    for block in range(NQ):
-        got(cols_sib.at[block], gs_recv.at[block])
-    lhs = jnp.concatenate([cols_sib[block] for block in range(NQ)], axis=1)
+
+    @pl.when(core == 0)
+    def _():
+        for block in range(NQ):
+            got(cols.at[1, block, 0], gs_recv.at[block])
+
+    lhs = jnp.concatenate([cols[1 - core, block, core] for block in range(NQ)], axis=1)
     total += jnp.dot(lhs, act_sib[...].reshape(NQ * 128, 768), preferred_element_type=jnp.float32)
     gw_ref[...] = total.astype(jnp.bfloat16)
 
@@ -271,7 +318,25 @@
 
     @pl.when(to_away)
     def _():
-        sent(grad_hbm, g_sem.at[0])
+        sent(grad_hbm, g_send)
+
+    @pl.when(core == 1)
+    def _():
+        ref = piece(0, cz, 0)
+        for par in range(2):
+            sent(ref, peer_send.at[par])
+            for n in range(2):
+                for step in range(NZ // 2):
+                    sent(ref, right_send.at[par, n, step])
+                    if step < NZ // 2 - 1:
+                        sent(ref, left_send.at[par, n, step])
+        whole = cols.at[0, 0, 0]
+        for step in range(NZ // 2 + 1):
+            sent(whole, hand_send.at[0, step])
+            if 0 < step < NZ // 2:
+                sent(whole, hand_send.at[1, step])
+        for step in range(NZ // 2):
+            sent(whole, gs_send.at[step])
 
     for copy in started:
         copy.wait_send()
@@ -296,8 +361,7 @@
         scratch_shapes=[
             pltpu.VMEM((128, 768), bf16),
             pltpu.VMEM((2, 768, 384), bf16),
-            pltpu.VMEM((NQ, 2, 384, 128), bf16),
-            pltpu.VMEM((NQ, 384, 128), bf16),
+            pltpu.VMEM((2, NQ, 2, 384, 128), bf16),
             pltpu.VMEM((NQ, 128, 768), bf16),
             pltpu.VMEM((NQ, 128, 768), bf16),
             pltpu.VMEM((128, 768), f32),
@@ -306,8 +370,9 @@
             pltpu.VMEM((NY - 1, 768, 128), bf16),
             pltpu.VMEM((NY, 768, 128), bf16),
             pltpu.VMEM((NY, 768, 128), bf16),
-            dma((2,)), dma((2,)), dma((2,)), dma((2,)),
-            dma((2, half)), dma((2, half)), dma((2, half)), dma((2, half)),
+            dma((2,)), dma((2,)), dma, dma((2,)), dma((2,)), dma((2,)),
+            dma((2, half + 1)), dma((2, half + 1)),
+            dma((2, 2, half)), dma((2, 2, half)), dma((2, 2, half)), dma((2, 2, half)),
             dma((half,)), dma((NQ,)), dma((2,)), dma((2, 2)), dma((2, 2)),
             dma((2, 2)), dma((2, 2)), dma((NQ,)), dma((NQ,)),
             dma((NY,)), dma((NY,)), dma((NY,)), dma((NY,)),

time: 72.9 us -> 74 us (1.015)
  the two profiles are of different devices: /device:TPU:8 before, /device:TPU:1 now
where the time goes in v3:
time: 74 us; the launch traced here: 73.8 us
  Pallas kernels  70.3 us (95%)
  local copies, waits for them, and re-layouts  2.84 us (4%)
    pallas_call x1, Pallas kernels, local(): pl.pallas_call(kernel, out_shape=(jax.ShapeDtypeStruct((128, 768), bf16),...  70.3 us
    unnamed x4, local copies, waits for them, and re-layouts  2.84 us

profile of v3, /device:TPU:1, one launch (start us, length us, event | category | flops | bytes accessed | tf_op | source)
XLA Modules:
  0.0 73.8 jit_solution(3290133455230812387)
XLA Ops:
  0.6 70.3 %shard_map.50 = (bf16[128,768]{1,0:T(8,128)(2,1)}, bf16[384,768]{1,0:T(8,128)(2,1)}) custom-call(bf16[128,768]{1,0:T(8,128)(2,1)} %hid_hbm.1, bf16[192,128]{1,0:T(8,128)(2,1)} %bitcast.3, bf16[768,384]{1,0:T(8,128)(2,1)} %w_hbm.1), custom_call_target="tpu_custom_call" | custom-call | tf_op jit(solution)/shard_map/pallas_call | solution.py:353
  71.0 0.0 copy-start
  71.0 2.2 %copy.5 = bf16[768,384]{1,0:T(8,128)(2,1)} copy(bf16[768,384]{0,1:T(8,128)(2,1)} %bitcast.2) | data formatting | bytes 1179648
  73.1 0.0 copy-done
  73.1 0.7 copy.7
Async XLA Ops:
  71.0 2.2 %copy-start = (bf16[128,768]{1,0:T(8,128)(2,1)S(1)}, bf16[128,768]{1,0:T(8,128)(2,1)}, u32[]{:S(2)}) copy-start(bf16[128,768]{1,0:T(8,128)(2,1)} %get-tuple-element.10) | copy-start | bytes 589828

commit v4 on v3

--- a/solution.py
+++ b/solution.py
@@ -25,10 +25,10 @@
 
 def kernel(
     hid_hbm, grad_hbm, w_hbm, gh_ref, gw_ref,
-    hid, wts, cols, act_own, act_sib, slope, first, second, comb, x_parts, y_parts,
+    hid, wts, cols, act_own, act_sib, slope, stage, parts,
     loc_sem, w_sem, g_send, g_recv, peer_send, peer_recv, hand_send, hand_recv, right_send, right_recv, left_send, left_recv,
     gs_send, gs_recv, ax_sem, ay_send, ay_recv, ah_send, ah_recv, as_send, as_recv,
-    x_send, x_recv, y_send, y_recv,
+    rs_send, rs_recv,
 ):
     rem, div = lax.rem, lax.div
     dp = lax.axis_index("dp")
@@ -65,19 +65,13 @@
     from_tn = chip * 4 + rem(cz, 2) * 2 + ch
     to_away = jnp.logical_or(to_dp != dp, to_tn != tn)
 
-    lead = div(cz, 4)
-    turn = 1 - 2 * rem(div(cz, 2), 2)
-    order = [lead, rem(lead + NY - turn, NY), rem(lead + NY + turn, NY), rem(lead + 2, NY)]
-    last = order[3]
-
     up = at(dp, ch * NZ + rem(cz + 1, NZ))
     down = at(dp, ch * NZ + rem(cz + NZ - 1, NZ))
     across = at(dp, rem(tn + NZ, 2 * NZ))
     beside = at(sib, tn)
 
     barrier = pltpu.get_barrier_semaphore()
-    greet = [beside, peer_at(0, 1), peer_at(NY - last, 1)]
-    greet += [peer_at(dy, 0) for dy in range(1, NY)]
+    greet = [beside] + [peer_at(j // NX, j % NX) for j in range(1, NQ)]
     for other in greet:
         pl.semaphore_signal(barrier, inc=1, device_id=other, device_id_type=MESH)
 
@@ -94,11 +88,6 @@
     cp_w = pltpu.make_async_copy(w_hbm, wts.at[core], loc_sem.at[1])
     cp_hid.start()
     cp_w.start()
-    cp_hid.wait()
-    act, slp = gelu_parts(hid[...].astype(jnp.float32))
-    act_own[chip] = act.astype(jnp.bfloat16)
-    slope[...] = slp
-    cp_w.wait()
     pl.semaphore_wait(barrier, len(greet) + 3 * core + to_away.astype(jnp.int32))
 
     started = []
@@ -158,7 +147,12 @@
             got(act_own.at[block, pl.ds(k * 64, 64)], ah_recv.at[dx, k])
         act_to_sib(2 * NX + dx)
 
+    cp_w.wait()
     send(wts.at[core], wts.at[core], w_sem.at[0], w_sem.at[1], beside)
+    cp_hid.wait()
+    act, slp = gelu_parts(hid[...].astype(jnp.float32))
+    act_own[chip] = act.astype(jnp.bfloat16)
+    slope[...] = slp
     send(act_own.at[chip], act_own.at[chip], ax_sem.at[0], ax_sem.at[1], peer_at(0, 1))
     act_to_y(0)
     act_to_sib(0)
@@ -240,38 +234,15 @@
         value = jnp.dot(wts[0], cols[core, block, 0], preferred_element_type=jnp.float32)
         value += jnp.dot(wts[1], cols[core, block, 1], preferred_element_type=jnp.float32)
         value = value.astype(jnp.bfloat16)
-        final = (dy == last).astype(jnp.int32)
-
-        @pl.when(dx == 1)
-        def _():
-            second[dy] = value
-            send(second.at[dy], x_parts.at[dy], x_send.at[dy], x_recv.at[dy], peer_at(final * dy, 1), keep=False)
-
-        @pl.when(jnp.logical_and(dx == 0, jnp.logical_or(final == 0, dy != 0)))
-        def _():
-            first[dy] = value
-
-        @pl.when(jnp.logical_and(jnp.logical_and(dx == 0, final == 1), dy != 0))
-        def _():
-            send(first.at[dy], y_parts.at[dy], y_send.at[dy], y_recv.at[dy], peer_at(dy, 0), keep=False)
-
-        @pl.when(jnp.logical_and(jnp.logical_and(dx == 0, final == 1), dy == 0))
-        def _():
-            y_parts[0] = value
-
-    def combine(i):
-        dy = order[i]
-        got(x_parts.at[dy], x_recv.at[dy])
-        value = (first[dy].astype(jnp.float32) + x_parts[dy].astype(jnp.float32)).astype(jnp.bfloat16)
-
-        @pl.when(dy == 0)
-        def _():
-            y_parts[0] = value
-
-        @pl.when(dy != 0)
-        def _():
-            comb[i] = value
-            send(comb.at[i], y_parts.at[dy], y_send.at[dy], y_recv.at[dy], peer_at(dy, 0), keep=False)
+
+        @pl.when(j == 0)
+        def _():
+            parts[0] = value
+
+        @pl.when(j != 0)
+        def _():
+            stage[step - 1] = value
+            send(stage.at[step - 1], parts.at[j], rs_send.at[j], rs_recv.at[j], peer_at(dy, dx), keep=False)
 
     for step in range(1, NZ // 2 + 1):
         ring(step)
@@ -283,16 +254,11 @@
         elif step == 2:
             act_from_y(0)
         elif step == 4:
-            combine(0)
             act_from_y(1)
         elif step == 5:
             act_halves(0)
-        elif step == 6:
-            combine(1)
         elif step == 7:
             act_halves(1)
-        elif step == 8:
-            combine(2)
 
     lhs = jnp.concatenate([cols[core, block, core] for block in range(NQ)], axis=1)
     total = jnp.dot(lhs, act_own[...].reshape(NQ * 128, 768), preferred_element_type=jnp.float32)
@@ -308,12 +274,11 @@
     total += jnp.dot(lhs, act_sib[...].reshape(NQ * 128, 768), preferred_element_type=jnp.float32)
     gw_ref[...] = total.astype(jnp.bfloat16)
 
-    for dy in range(1, NY):
-        got(y_parts.at[dy], y_recv.at[dy])
-    got(x_parts.at[last], x_recv.at[last])
-    summed = x_parts[last].astype(jnp.float32)
-    for dy in range(NY):
-        summed += y_parts[dy].astype(jnp.float32)
+    for j in range(1, NQ):
+        got(parts.at[j], rs_recv.at[j])
+    summed = parts[0].astype(jnp.float32)
+    for j in range(1, NQ):
+        summed += parts[j].astype(jnp.float32)
     gh_ref[...] = (slope[...] * summed.T).astype(jnp.bfloat16)
 
     @pl.when(to_away)
@@ -340,10 +305,8 @@
 
     for copy in started:
         copy.wait_send()
-    for dy in range(NY):
-        sent(second.at[dy], x_send.at[dy])
-    for dy in range(1, NY):
-        sent(comb.at[0], y_send.at[dy])
+    for j in range(1, NQ):
+        sent(stage.at[0], rs_send.at[j])
 
 
 def local(hidden_pre, out_grad, down_weight):
@@ -365,17 +328,14 @@
             pltpu.VMEM((NQ, 128, 768), bf16),
             pltpu.VMEM((NQ, 128, 768), bf16),
             pltpu.VMEM((128, 768), f32),
-            pltpu.VMEM((NY, 768, 128), bf16),
-            pltpu.VMEM((NY, 768, 128), bf16),
-            pltpu.VMEM((NY - 1, 768, 128), bf16),
-            pltpu.VMEM((NY, 768, 128), bf16),
-            pltpu.VMEM((NY, 768, 128), bf16),
+            pltpu.VMEM((NQ, 768, 128), bf16),
+            pltpu.VMEM((NQ, 768, 128), bf16),
             dma((2,)), dma((2,)), dma, dma((2,)), dma((2,)), dma((2,)),
             dma((2, half + 1)), dma((2, half + 1)),
             dma((2, 2, half)), dma((2, 2, half)), dma((2, 2, half)), dma((2, 2, half)),
             dma((half,)), dma((NQ,)), dma((2,)), dma((2, 2)), dma((2, 2)),
             dma((2, 2)), dma((2, 2)), dma((NQ,)), dma((NQ,)),
-            dma((NY,)), dma((NY,)), dma((NY,)), dma((NY,)),
+            dma((NQ,)), dma((NQ,)),
         ],
         compiler_params=pltpu.CompilerParams(
             collective_id=0, has_side_effects=True, vmem_limit_bytes=60 * 1024 * 1024

time: 74 us -> 80.7 us (1.091)
  the two profiles are of different devices: /device:TPU:1 before, /device:TPU:8 now
where the time goes in v4:
time: 80.7 us; the launch traced here: 80.5 us
  Pallas kernels  77 us (95%)
  local copies, waits for them, and re-layouts  2.84 us (4%)
    pallas_call x1, Pallas kernels, local(): pl.pallas_call(kernel, out_shape=(jax.ShapeDtypeStruct((128, 768), bf16),...  77 us
    unnamed x4, local copies, waits for them, and re-layouts  2.84 us

profile of v4, /device:TPU:8, one launch (start us, length us, event | category | flops | bytes accessed | tf_op | source)
XLA Modules:
  0.0 80.5 jit_solution(871890615915133697)
XLA Ops:
  0.6 77.0 %shard_map.50 = (bf16[128,768]{1,0:T(8,128)(2,1)}, bf16[384,768]{1,0:T(8,128)(2,1)}) custom-call(bf16[128,768]{1,0:T(8,128)(2,1)} %hid_hbm.1, bf16[192,128]{1,0:T(8,128)(2,1)} %bitcast.3, bf16[768,384]{1,0:T(8,128)(2,1)} %w_hbm.1), custom_call_target="tpu_custom_call" | custom-call | tf_op jit(solution)/shard_map/pallas_call | solution.py:316
  77.6 0.0 copy-start
  77.6 2.2 %copy.5 = bf16[768,384]{1,0:T(8,128)(2,1)} copy(bf16[768,384]{0,1:T(8,128)(2,1)} %bitcast.2) | data formatting | bytes 1179648
  79.8 0.0 copy-done
  79.8 0.7 copy.7
Async XLA Ops:
  77.6 2.2 %copy-start = (bf16[128,768]{1,0:T(8,128)(2,1)S(1)}, bf16[128,768]{1,0:T(8,128)(2,1)}, u32[]{:S(2)}) copy-start(bf16[128,768]{1,0:T(8,128)(2,1)} %get-tuple-element.10) | copy-start | bytes 589828

commit v5 on v4

--- a/solution.py
+++ b/solution.py
@@ -50,18 +50,21 @@
     def peer_at(dy, dx):
         return at(chip_at(dy, dx) * 2 + core, tn)
 
-    def slot_at(place):
-        return block_at(div(place, 2)), rem(place, 2)
+    def shift(j, par):
+        return rem(div(j, NX) + 2 * par, NY), rem(j + par, NX)
+
+    def slot_at(place, par):
+        return chip_at(*shift(div(place, 2), par)), rem(place, 2)
 
     def piece(par, place, part):
-        block, half = slot_at(place)
+        block, half = slot_at(place, par)
         return cols.at[par, block, half, pl.ds(pl.multiple_of(part * 192, 64), 192)]
 
     to_chip, to_half, to_part = div(tn, 4), rem(div(tn, 2), 2), rem(tn, 2)
-    to_j = rem(cy - div(to_chip, NX) + NY, NY) * NX + rem(cx - rem(to_chip, NX) + NX, NX)
+    to_j = rem(cy - div(to_chip, NX) + NY + 2 * core, NY) * NX + rem(cx - rem(to_chip, NX) + NX + core, NX)
     to_dp = to_chip * 2 + 1
     to_tn = to_part * NZ + to_j * 2 + to_half
-    from_dp = slot_at(cz)[0] * 2
+    from_dp = [slot_at(cz, par)[0] * 2 + par for par in range(2)]
     from_tn = chip * 4 + rem(cz, 2) * 2 + ch
     to_away = jnp.logical_or(to_dp != dp, to_tn != tn)
 
@@ -77,12 +80,12 @@
 
     @pl.when(core == 1)
     def _():
-        for other in (up, down, across, at(from_dp, from_tn)):
+        for other in (up, down, across, at(from_dp[0], from_tn)):
             pl.semaphore_signal(barrier, inc=1, device_id=other, device_id_type=MESH)
 
-        @pl.when(jnp.logical_or(from_dp + 1 != dp, from_tn != tn))
-        def _():
-            pl.semaphore_signal(barrier, inc=1, device_id=at(from_dp + 1, from_tn), device_id_type=MESH)
+        @pl.when(jnp.logical_or(from_dp[1] != dp, from_tn != tn))
+        def _():
+            pl.semaphore_signal(barrier, inc=1, device_id=at(from_dp[1], from_tn), device_id_type=MESH)
 
     cp_hid = pltpu.make_async_copy(hid_hbm, hid, loc_sem.at[0])
     cp_w = pltpu.make_async_copy(w_hbm, wts.at[core], loc_sem.at[1])
@@ -174,12 +177,12 @@
             send(ref, ref, left_send.at[par, n, step], left_recv.at[par, n, step], down, keep=False)
 
     def hand(way, step):
-        block, half = slot_at(rem(cz + NZ + (step if way else -step), NZ))
+        block, half = slot_at(rem(cz + NZ + (step if way else -step), NZ), 0)
         ref = cols.at[0, block, half]
         send(ref, ref, hand_send.at[way, step], hand_recv.at[way, step], beside, keep=False)
 
     def handed(way, step):
-        block, half = slot_at(rem(cz + NZ + (step if way else -step), NZ))
+        block, half = slot_at(rem(cz + NZ + (step if way else -step), NZ), 0)
         got(cols.at[0, block, half], hand_recv.at[way, step])
 
     def ring(step):
@@ -199,6 +202,11 @@
             handed(0, step)
             if step < NZ // 2:
                 handed(1, step)
+
+    got(act_own.at[chip_at(0, 1)], ax_sem.at[1])
+    act_to_y(1)
+    act_to_sib(1)
+    act_from_y(0)
 
     @pl.when(core == 1)
     def _():
@@ -221,8 +229,9 @@
     def partial(step):
         odd = rem(cz + step, 2)
         j = div(rem(cz + NZ + jnp.where(odd == 1, step, -step), NZ), 2)
-        dy, dx = div(j, NX), rem(j, NX)
-        block = block_at(j)
+        dy, dx = shift(j, core)
+        block = chip_at(dy, dx)
+        j = dy * NX + dx
 
         @pl.when(core == 1)
         def _():
@@ -248,16 +257,10 @@
         ring(step)
         partial(step)
         if step == 1:
-            got(act_own.at[chip_at(0, 1)], ax_sem.at[1])
-            act_to_y(1)
-            act_to_sib(1)
+            act_from_y(1)
         elif step == 2:
-            act_from_y(0)
-        elif step == 4:
-            act_from_y(1)
-        elif step == 5:
             act_halves(0)
-        elif step == 7:
+        elif step == 3:
             act_halves(1)
 
     lhs = jnp.concatenate([cols[core, block, core] for block in range(NQ)], axis=1)

time: 80.7 us -> 68.1 us (0.84)
  the two profiles are of different devices: /device:TPU:8 before, /device:TPU:56 now
where the time goes in v5:
time: 68.1 us; the launch traced here: 67.9 us
  Pallas kernels  64.4 us (95%)
  local copies, waits for them, and re-layouts  2.84 us (4%)
    pallas_call x1, Pallas kernels, local(): pl.pallas_call(kernel, out_shape=(jax.ShapeDtypeStruct((128, 768), bf16),...  64.4 us
    unnamed x4, local copies, waits for them, and re-layouts  2.84 us

profile of v5, /device:TPU:56, one launch (start us, length us, event | category | flops | bytes accessed | tf_op | source)
XLA Modules:
  0.0 67.9 jit_solution(10933857156697912767)
XLA Ops:
  0.6 64.4 %shard_map.50 = (bf16[128,768]{1,0:T(8,128)(2,1)}, bf16[384,768]{1,0:T(8,128)(2,1)}) custom-call(bf16[128,768]{1,0:T(8,128)(2,1)} %hid_hbm.1, bf16[192,128]{1,0:T(8,128)(2,1)} %bitcast.3, bf16[768,384]{1,0:T(8,128)(2,1)} %w_hbm.1), custom_call_target="tpu_custom_call" | custom-call | tf_op jit(solution)/shard_map/pallas_call | solution.py:319
  65.0 0.0 copy-start
  65.1 2.2 %copy.5 = bf16[768,384]{1,0:T(8,128)(2,1)} copy(bf16[768,384]{0,1:T(8,128)(2,1)} %bitcast.2) | data formatting | bytes 1179648
  67.2 0.0 copy-done
  67.2 0.7 copy.7
Async XLA Ops:
  65.0 2.2 %copy-start = (bf16[128,768]{1,0:T(8,128)(2,1)S(1)}, bf16[128,768]{1,0:T(8,128)(2,1)}, u32[]{:S(2)}) copy-start(bf16[128,768]{1,0:T(8,128)(2,1)} %get-tuple-element.10) | copy-start | bytes 589828

commit v6 on v5

--- a/solution.py
+++ b/solution.py
@@ -25,9 +25,9 @@
 
 def kernel(
     hid_hbm, grad_hbm, w_hbm, gh_ref, gw_ref,
-    hid, wts, cols, act_own, act_sib, slope, stage, parts,
+    hid, wts, cols, acts, slope, stage, parts,
     loc_sem, w_sem, g_send, g_recv, peer_send, peer_recv, hand_send, hand_recv, right_send, right_recv, left_send, left_recv,
-    gs_send, gs_recv, ax_sem, ay_send, ay_recv, ah_send, ah_recv, as_send, as_recv,
+    gs_send, gs_recv, own_send, own_recv, ax_sem, ay_send, ay_recv, ah_send, ah_recv, as_send, as_recv,
     rs_send, rs_recv,
 ):
     rem, div = lax.rem, lax.div
@@ -74,18 +74,20 @@
     beside = at(sib, tn)
 
     barrier = pltpu.get_barrier_semaphore()
+    @pl.when(core == 1)
+    def _():
+        pl.semaphore_signal(barrier, inc=1, device_id=at(from_dp[0], from_tn), device_id_type=MESH)
+
+        @pl.when(jnp.logical_or(from_dp[1] != dp, from_tn != tn))
+        def _():
+            pl.semaphore_signal(barrier, inc=1, device_id=at(from_dp[1], from_tn), device_id_type=MESH)
+
+        for other in (up, down, across):
+            pl.semaphore_signal(barrier, inc=1, device_id=other, device_id_type=MESH)
+
     greet = [beside] + [peer_at(j // NX, j % NX) for j in range(1, NQ)]
     for other in greet:
         pl.semaphore_signal(barrier, inc=1, device_id=other, device_id_type=MESH)
-
-    @pl.when(core == 1)
-    def _():
-        for other in (up, down, across, at(from_dp[0], from_tn)):
-            pl.semaphore_signal(barrier, inc=1, device_id=other, device_id_type=MESH)
-
-        @pl.when(jnp.logical_or(from_dp[1] != dp, from_tn != tn))
-        def _():
-            pl.semaphore_signal(barrier, inc=1, device_id=at(from_dp[1], from_tn), device_id_type=MESH)
 
     cp_hid = pltpu.make_async_copy(hid_hbm, hid, loc_sem.at[0])
     cp_w = pltpu.make_async_copy(w_hbm, wts.at[core], loc_sem.at[1])
@@ -129,36 +131,44 @@
     def act_to_y(dx):
         block = chip_at(0, dx)
         for k, dy in ((0, 1), (1, NY - 1)):
-            send(act_own.at[block], act_own.at[block], ay_send.at[dx, k], ay_recv.at[dx, k], peer_at(dy, 0))
+            send(acts.at[block], acts.at[block], ay_send.at[dx, k], ay_recv.at[dx, k], peer_at(dy, 0), keep=False)
 
     def act_to_sib(j):
         block = block_at(j)
-        send(act_own.at[block], act_sib.at[block], as_send.at[j], as_recv.at[j], beside)
+        send(acts.at[block], acts.at[block], as_send.at[j], as_recv.at[j], beside, keep=False)
 
     def act_from_y(dx):
         for k, dy in ((0, NY - 1), (1, 1)):
             block = chip_at(dy, dx)
-            got(act_own.at[block], ay_recv.at[dx, k])
-            rows = pl.ds(k * 64, 64)
-            send(act_own.at[block, rows], act_own.at[block, rows],
-                 ah_send.at[dx, k], ah_recv.at[dx, k], peer_at(NY - dy, 0))
+            got(acts.at[block], ay_recv.at[dx, k])
+            send(acts.at[block, k], acts.at[block, k],
+                 ah_send.at[dx, k], ah_recv.at[dx, k], peer_at(NY - dy, 0), keep=False)
             act_to_sib(dy * NX + dx)
 
     def act_halves(dx):
         block = chip_at(2, dx)
         for k in range(2):
-            got(act_own.at[block, pl.ds(k * 64, 64)], ah_recv.at[dx, k])
+            got(acts.at[block, k], ah_recv.at[dx, k])
         act_to_sib(2 * NX + dx)
+
+    def act_from_x():
+        got(acts.at[chip_at(0, 1)], ax_sem.at[1])
+        act_to_y(1)
+        act_to_sib(1)
 
     cp_w.wait()
     send(wts.at[core], wts.at[core], w_sem.at[0], w_sem.at[1], beside)
     cp_hid.wait()
     act, slp = gelu_parts(hid[...].astype(jnp.float32))
-    act_own[chip] = act.astype(jnp.bfloat16)
+    acts[chip, core] = act.astype(jnp.bfloat16)
     slope[...] = slp
-    send(act_own.at[chip], act_own.at[chip], ax_sem.at[0], ax_sem.at[1], peer_at(0, 1))
-    act_to_y(0)
-    act_to_sib(0)
+    send(acts.at[chip, core], acts.at[chip, core], own_send, own_recv, beside)
+
+    @pl.when(core == 0)
+    def _():
+        got(acts.at[chip, 1], own_recv)
+        send(acts.at[chip], acts.at[chip], ax_sem.at[0], ax_sem.at[1], peer_at(0, 1), keep=False)
+        act_to_y(0)
 
     pieces = (ch, 1 - ch)
 
@@ -166,14 +176,14 @@
         ref = piece(par, rem(cz + NZ - step, NZ), pieces[n])
         if step > 0:
             got(ref, right_recv.at[par, n, step - 1])
-        if step < NZ // 2:
+        if step < NZ // 2 - n:
             send(ref, ref, right_send.at[par, n, step], right_recv.at[par, n, step], up, keep=False)
 
     def left(step, n, par):
         ref = piece(par, rem(cz + step, NZ), pieces[n])
         if step > 0:
             got(ref, left_recv.at[par, n, step - 1])
-        if step < NZ // 2 - 1:
+        if step < NZ // 2 - 1 + n:
             send(ref, ref, left_send.at[par, n, step], left_recv.at[par, n, step], down, keep=False)
 
     def hand(way, step):
@@ -190,8 +200,9 @@
         def _():
             for n in range(2):
                 for par in range(2):
-                    right(step, n, par)
-                    if step < NZ // 2:
+                    if step <= NZ // 2 - n:
+                        right(step, n, par)
+                    if step < NZ // 2 + n:
                         left(step, n, par)
             hand(0, step)
             if step < NZ // 2:
@@ -203,10 +214,11 @@
             if step < NZ // 2:
                 handed(1, step)
 
-    got(act_own.at[chip_at(0, 1)], ax_sem.at[1])
-    act_to_y(1)
-    act_to_sib(1)
-    act_from_y(0)
+    @pl.when(core == 0)
+    def _():
+        act_from_x()
+        act_from_y(0)
+        act_from_y(1)
 
     @pl.when(core == 1)
     def _():
@@ -256,25 +268,24 @@
     for step in range(1, NZ // 2 + 1):
         ring(step)
         partial(step)
-        if step == 1:
-            act_from_y(1)
-        elif step == 2:
-            act_halves(0)
-        elif step == 3:
-            act_halves(1)
-
-    lhs = jnp.concatenate([cols[core, block, core] for block in range(NQ)], axis=1)
-    total = jnp.dot(lhs, act_own[...].reshape(NQ * 128, 768), preferred_element_type=jnp.float32)
-    for j in range(NQ):
-        got(act_sib.at[block_at(j)], as_recv.at[j])
+        if step <= 2:
+            @pl.when(core == 0)
+            def _():
+                act_halves(step - 1)
+
+    @pl.when(core == 1)
+    def _():
+        got(acts.at[chip, 0], own_recv)
+        for j in range(1, NQ):
+            got(acts.at[block_at(j)], as_recv.at[j])
 
     @pl.when(core == 0)
     def _():
         for block in range(NQ):
             got(cols.at[1, block, 0], gs_recv.at[block])
 
-    lhs = jnp.concatenate([cols[1 - core, block, core] for block in range(NQ)], axis=1)
-    total += jnp.dot(lhs, act_sib[...].reshape(NQ * 128, 768), preferred_element_type=jnp.float32)
+    lhs = jnp.concatenate([cols[par, block, core] for block in range(NQ) for par in range(2)], axis=1)
+    total = jnp.dot(lhs, acts[...].reshape(NQ * 256, 768), preferred_element_type=jnp.float32)
     gw_ref[...] = total.astype(jnp.bfloat16)
 
     for j in range(1, NQ):
@@ -295,8 +306,9 @@
             sent(ref, peer_send.at[par])
             for n in range(2):
                 for step in range(NZ // 2):
-                    sent(ref, right_send.at[par, n, step])
-                    if step < NZ // 2 - 1:
+                    if step < NZ // 2 - n:
+                        sent(ref, right_send.at[par, n, step])
+                    if step < NZ // 2 - 1 + n:
                         sent(ref, left_send.at[par, n, step])
         whole = cols.at[0, 0, 0]
         for step in range(NZ // 2 + 1):
@@ -308,6 +320,17 @@
 
     for copy in started:
         copy.wait_send()
+
+    @pl.when(core == 0)
+    def _():
+        sent(acts.at[0], ax_sem.at[0])
+        for dx in range(2):
+            for k in range(2):
+                sent(acts.at[0], ay_send.at[dx, k])
+                sent(acts.at[0, 0], ah_send.at[dx, k])
+        for j in range(1, NQ):
+            sent(acts.at[0], as_send.at[j])
+
     for j in range(1, NQ):
         sent(stage.at[0], rs_send.at[j])
 
@@ -328,15 +351,14 @@
             pltpu.VMEM((128, 768), bf16),
             pltpu.VMEM((2, 768, 384), bf16),
             pltpu.VMEM((2, NQ, 2, 384, 128), bf16),
-            pltpu.VMEM((NQ, 128, 768), bf16),
-            pltpu.VMEM((NQ, 128, 768), bf16),
+            pltpu.VMEM((NQ, 2, 128, 768), bf16),
             pltpu.VMEM((128, 768), f32),
             pltpu.VMEM((NQ, 768, 128), bf16),
             pltpu.VMEM((NQ, 768, 128), bf16),
             dma((2,)), dma((2,)), dma, dma((2,)), dma((2,)), dma((2,)),
             dma((2, half + 1)), dma((2, half + 1)),
             dma((2, 2, half)), dma((2, 2, half)), dma((2, 2, half)), dma((2, 2, half)),
-            dma((half,)), dma((NQ,)), dma((2,)), dma((2, 2)), dma((2, 2)),
+            dma((half,)), dma((NQ,)), dma, dma, dma((2,)), dma((2, 2)), dma((2, 2)),
             dma((2, 2)), dma((2, 2)), dma((NQ,)), dma((NQ,)),
             dma((NQ,)), dma((NQ,)),
         ],

time: 68.1 us -> 65.7 us (0.965)
  the two profiles are of different devices: /device:TPU:56 before, /device:TPU:1 now
where the time goes in v6:
time: 65.7 us; the launch traced here: 65.4 us
  Pallas kernels  61.9 us (94%)
  local copies, waits for them, and re-layouts  2.84 us (4%)
    pallas_call x1, Pallas kernels, local(): pl.pallas_call(kernel, out_shape=(jax.ShapeDtypeStruct((128, 768), bf16),...  61.9 us
    unnamed x4, local copies, waits for them, and re-layouts  2.84 us

profile of v6, /device:TPU:1, one launch (start us, length us, event | category | flops | bytes accessed | tf_op | source)
XLA Modules:
  0.0 65.4 jit_solution(9155898672981049432)
XLA Ops:
  0.6 61.9 %shard_map.50 = (bf16[128,768]{1,0:T(8,128)(2,1)}, bf16[384,768]{1,0:T(8,128)(2,1)}) custom-call(bf16[128,768]{1,0:T(8,128)(2,1)} %hid_hbm.1, bf16[192,128]{1,0:T(8,128)(2,1)} %bitcast.3, bf16[768,384]{1,0:T(8,128)(2,1)} %w_hbm.1), custom_call_target="tpu_custom_call" | custom-call | tf_op jit(solution)/shard_map/pallas_call | solution.py:342
  62.5 0.0 copy-start
  62.5 2.2 %copy.5 = bf16[768,384]{1,0:T(8,128)(2,1)} copy(bf16[768,384]{0,1:T(8,128)(2,1)} %bitcast.2) | data formatting | bytes 1179648
  64.7 0.0 copy-done
  64.7 0.7 %copy.7 = bf16[128,768]{1,0:T(8,128)(2,1)} copy(bf16[128,768]{1,0:T(8,128)(2,1)S(1)} %copy-done) | data formatting | bytes 393216
Async XLA Ops:
  62.5 2.2 %copy-start = (bf16[128,768]{1,0:T(8,128)(2,1)S(1)}, bf16[128,768]{1,0:T(8,128)(2,1)}, u32[]{:S(2)}) copy-start(bf16[128,768]{1,0:T(8,128)(2,1)} %get-tuple-element.10) | copy-start | bytes 589828

commit v7 on v6

--- a/solution.py
+++ b/solution.py
@@ -156,19 +156,19 @@
         act_to_y(1)
         act_to_sib(1)
 
+    cp_hid.wait()
+    acts[chip, core] = gelu_parts(hid[...].astype(jnp.float32))[0].astype(jnp.bfloat16)
+    send(acts.at[chip, core], acts.at[chip, core], own_send, own_recv, beside)
     cp_w.wait()
-    send(wts.at[core], wts.at[core], w_sem.at[0], w_sem.at[1], beside)
-    cp_hid.wait()
-    act, slp = gelu_parts(hid[...].astype(jnp.float32))
-    acts[chip, core] = act.astype(jnp.bfloat16)
-    slope[...] = slp
-    send(acts.at[chip, core], acts.at[chip, core], own_send, own_recv, beside)
 
     @pl.when(core == 0)
     def _():
         got(acts.at[chip, 1], own_recv)
         send(acts.at[chip], acts.at[chip], ax_sem.at[0], ax_sem.at[1], peer_at(0, 1), keep=False)
         act_to_y(0)
+
+    send(wts.at[core], wts.at[core], w_sem.at[0], w_sem.at[1], beside)
+    slope[...] = gelu_parts(hid[...].astype(jnp.float32))[1]
 
     pieces = (ch, 1 - ch)
 
@@ -252,18 +252,22 @@
 
         if step == 1:
             got(wts.at[1 - core], w_sem.at[1])
-        value = jnp.dot(wts[0], cols[core, block, 0], preferred_element_type=jnp.float32)
-        value += jnp.dot(wts[1], cols[core, block, 1], preferred_element_type=jnp.float32)
-        value = value.astype(jnp.bfloat16)
-
-        @pl.when(j == 0)
-        def _():
-            parts[0] = value
-
-        @pl.when(j != 0)
-        def _():
-            stage[step - 1] = value
-            send(stage.at[step - 1], parts.at[j], rs_send.at[j], rs_recv.at[j], peer_at(dy, dx), keep=False)
+        rows = 384 if step == NZ // 2 else 768
+        for at_row in range(0, 768, rows):
+            some = pl.ds(at_row, rows)
+            value = jnp.dot(wts[0, some], cols[core, block, 0], preferred_element_type=jnp.float32)
+            value += jnp.dot(wts[1, some], cols[core, block, 1], preferred_element_type=jnp.float32)
+            value = value.astype(jnp.bfloat16)
+
+            @pl.when(j == 0)
+            def _():
+                parts[0, some] = value
+
+            @pl.when(j != 0)
+            def _():
+                stage[step - 1, some] = value
+                send(stage.at[step - 1, some], parts.at[j, some], rs_send.at[j], rs_recv.at[j],
+                     peer_at(dy, dx), keep=False)
 
     for step in range(1, NZ // 2 + 1):
         ring(step)

time: 65.7 us -> 65.8 us (level)
  no operation moved by 1% of the time
where the time goes in v7:
time: 65.8 us; the launch traced here: 65.3 us
  Pallas kernels  61.8 us (94%)
  local copies, waits for them, and re-layouts  2.84 us (4%)
    pallas_call x1, Pallas kernels, local(): pl.pallas_call(kernel, out_shape=(jax.ShapeDtypeStruct((128, 768), bf16),...  61.8 us
    unnamed x4, local copies, waits for them, and re-layouts  2.84 us

profile of v7, /device:TPU:1, one launch (start us, length us, event | category | flops | bytes accessed | tf_op | source)
XLA Modules:
  0.0 65.3 jit_solution(1827524267850043847)
XLA Ops:
  0.6 61.8 %shard_map.50 = (bf16[128,768]{1,0:T(8,128)(2,1)}, bf16[384,768]{1,0:T(8,128)(2,1)}) custom-call(bf16[128,768]{1,0:T(8,128)(2,1)} %hid_hbm.1, bf16[192,128]{1,0:T(8,128)(2,1)} %bitcast.3, bf16[768,384]{1,0:T(8,128)(2,1)} %w_hbm.1), custom_call_target="tpu_custom_call" | custom-call | tf_op jit(solution)/shard_map/pallas_call | solution.py:346
  62.5 0.0 copy-start
  62.5 2.2 %copy.5 = bf16[768,384]{1,0:T(8,128)(2,1)} copy(bf16[768,384]{0,1:T(8,128)(2,1)} %bitcast.2) | data formatting | bytes 1179648
  64.6 0.0 copy-done
  64.7 0.7 %copy.7 = bf16[128,768]{1,0:T(8,128)(2,1)} copy(bf16[128,768]{1,0:T(8,128)(2,1)S(1)} %copy-done) | data formatting | bytes 393216
Async XLA Ops:
  62.5 2.2 %copy-start = (bf16[128,768]{1,0:T(8,128)(2,1)S(1)}, bf16[128,768]{1,0:T(8,128)(2,1)}, u32[]{:S(2)}) copy-start(bf16[128,768]{1,0:T(8,128)(2,1)} %get-tuple-element.10) | copy-start | bytes 589828

commit v8 on v6

--- a/solution.py
+++ b/solution.py
@@ -53,8 +53,11 @@
     def shift(j, par):
         return rem(div(j, NX) + 2 * par, NY), rem(j + par, NX)
 
+    def turned(place, y):
+        return rem(place + 6 + 8 * rem(y, 2), NZ)
+
     def slot_at(place, par):
-        return chip_at(*shift(div(place, 2), par)), rem(place, 2)
+        return chip_at(*shift(div(turned(place, cy), 2), par)), rem(place, 2)
 
     def piece(par, place, part):
         block, half = slot_at(place, par)
@@ -63,7 +66,8 @@
     to_chip, to_half, to_part = div(tn, 4), rem(div(tn, 2), 2), rem(tn, 2)
     to_j = rem(cy - div(to_chip, NX) + NY + 2 * core, NY) * NX + rem(cx - rem(to_chip, NX) + NX + core, NX)
     to_dp = to_chip * 2 + 1
-    to_tn = to_part * NZ + to_j * 2 + to_half
+    to_z = rem(to_j * 2 + to_half + 2 + 8 * rem(div(to_chip, NX) + 1, 2), NZ)
+    to_tn = to_part * NZ + to_z
     from_dp = [slot_at(cz, par)[0] * 2 + par for par in range(2)]
     from_tn = chip * 4 + rem(cz, 2) * 2 + ch
     to_away = jnp.logical_or(to_dp != dp, to_tn != tn)
@@ -240,7 +244,7 @@
 
     def partial(step):
         odd = rem(cz + step, 2)
-        j = div(rem(cz + NZ + jnp.where(odd == 1, step, -step), NZ), 2)
+        j = div(turned(rem(cz + NZ + jnp.where(odd == 1, step, -step), NZ), cy), 2)
         dy, dx = shift(j, core)
         block = chip_at(dy, dx)
         j = dy * NX + dx

time: 65.7 us -> 65.5 us (level)
  the two profiles are of different devices: /device:TPU:1 before, /device:TPU:118 now
where the time goes in v8:
time: 65.5 us; the launch traced here: 65.3 us
  Pallas kernels  61.9 us (95%)
  local copies, waits for them, and re-layouts  2.84 us (4%)
    pallas_call x1, Pallas kernels, local(): pl.pallas_call(kernel, out_shape=(jax.ShapeDtypeStruct((128, 768), bf16),...  61.9 us
    unnamed x4, local copies, waits for them, and re-layouts  2.84 us

profile of v8, /device:TPU:118, one launch (start us, length us, event | category | flops | bytes accessed | tf_op | source)
XLA Modules:
  0.0 65.3 jit_solution(4405601109650120726)
XLA Ops:
  0.6 61.9 %shard_map.50 = (bf16[128,768]{1,0:T(8,128)(2,1)}, bf16[384,768]{1,0:T(8,128)(2,1)}) custom-call(bf16[128,768]{1,0:T(8,128)(2,1)} %hid_hbm.1, bf16[192,128]{1,0:T(8,128)(2,1)} %bitcast.3, bf16[768,384]{1,0:T(8,128)(2,1)} %w_hbm.1), custom_call_target="tpu_custom_call" | custom-call | tf_op jit(solution)/shard_map/pallas_call | solution.py:346
  62.5 0.0 copy-start
  62.5 2.2 %copy.5 = bf16[768,384]{1,0:T(8,128)(2,1)} copy(bf16[768,384]{0,1:T(8,128)(2,1)} %bitcast.2) | data formatting | bytes 1179648
  64.7 0.0 copy-done
  64.7 0.7 %copy.7 = bf16[128,768]{1,0:T(8,128)(2,1)} copy(bf16[128,768]{1,0:T(8,128)(2,1)S(1)} %copy-done) | data formatting | bytes 393216
Async XLA Ops:
  62.5 2.2 %copy-start = (bf16[128,768]{1,0:T(8,128)(2,1)S(1)}, bf16[128,768]{1,0:T(8,128)(2,1)}, u32[]{:S(2)}) copy-start(bf16[128,768]{1,0:T(8,128)(2,1)} %get-tuple-element.10) | copy-start | bytes 589828
